TPU v7x, 32 devices: a whole 2x2x4 slice. The times are simulated.
32 devices in a mesh: tm: 4 (over x, core), height: 8 (over z, y).
Axes of the slice: x: 2, y: 2, z: 4, core: 2. Of those that a mesh axis runs over, the one named last changes fastest.
Arguments:
- clip: bfloat16 [8, 32, 64, 256], P('tm', 'height'), may hold values from -6 to 6
- cotangent: bfloat16 [8, 32, 64, 256], P('tm', 'height'), may hold values from -6 to 6
- spatial_weight: bfloat16 [3, 3, 256, 256], replicated, may hold values from -0.125 to 0.125
- temporal_weight: bfloat16 [3, 256, 256], replicated, may hold values from -0.21875 to 0.21875
Outputs:
- output: bfloat16 [8, 32, 64, 256], P('tm', 'height')
- grad_clip: bfloat16 [8, 32, 64, 256], P('tm', 'height')
- grad_spatial: float32 [589824], P(('tm', 'height'))
- grad_temporal: float32 [196608], P(('tm', 'height'))
All inputs are finite; a program needn't handle non-finite values.
Results may differ from a plain program's by a relative error of at most 0.0049.
Values may be sent and summed in bfloat16 or wider, within the bound.
A program may use at most 64 MiB of HBM per device.

v0:
```python
import math

import jax
import jax.numpy as jnp
from jax import lax
from jax.sharding import PartitionSpec as P

EPSILON = 1e-06


def extended(cells, sides, width):
    for axis, dim in sides:
        count = lax.axis_size(axis)
        ends = count - 1
        head = lax.slice_in_dim(cells, 0, width, axis=dim)
        tail = lax.slice_in_dim(cells, cells.shape[dim] - width, cells.shape[dim], axis=dim)
        cells = jnp.concatenate(
            [
                lax.ppermute(tail, axis, [(i, (i + 1) % count) for i in range(ends)]),
                cells,
                lax.ppermute(head, axis, [((i + 1) % count, i) for i in range(ends)]),
            ],
            axis=dim,
        )
    return cells


def shifted(block, axis, distance):
    devices = range(lax.axis_size(axis))
    route = [(i - distance, i) for i in devices if i - distance in devices]
    return lax.ppermute(block, axis, route)


def activate(values):
    scale_inv = lax.rsqrt(jnp.mean(values * values, axis=-1, keepdims=True) + EPSILON)
    return jax.nn.silu(values * scale_inv)


def flat_dot(left, weight):
    keep_shape = left.shape[:-1]
    result = jnp.dot(left.reshape(-1, left.shape[-1]), weight, preferred_element_type=jnp.float32)
    return result.reshape(keep_shape + (weight.shape[-1],))


def outer_sum(left, right):
    channels = left.shape[-1]
    return lax.dot_general(
        left.reshape(-1, channels),
        right.reshape(-1, channels),
        (((0,), (0,)), ((), ())),
        preferred_element_type=jnp.float32,
    )


def shards(clip, cotangent, spatial_weight, temporal_weight):
    frame_count, row_count, col_count, channels = clip.shape
    clip_wide = clip.astype(jnp.float32)
    activated = activate(clip_wide).astype(jnp.bfloat16)
    act_ext = extended(activated, (("height", 1),), 1)
    padded = jnp.pad(act_ext, ((0, 0), (0, 0), (1, 1), (0, 0)))
    spatial = jnp.zeros(clip.shape, jnp.float32)
    for tap_row in range(3):
        for tap_col in range(3):
            spatial = spatial + flat_dot(
                padded[:, tap_row : tap_row + row_count, tap_col : tap_col + col_count],
                spatial_weight[tap_row, tap_col],
            )
    middle = spatial.astype(jnp.bfloat16)
    earlier = shifted(middle, "tm", 1)
    history = jnp.concatenate([earlier, middle], axis=0)
    temporal = jnp.zeros(clip.shape, jnp.float32)
    for time_lag in range(3):
        temporal = temporal + flat_dot(
            history[2 - time_lag : 2 - time_lag + frame_count], temporal_weight[time_lag]
        )
    output = (clip_wide + temporal).astype(jnp.bfloat16)
    later = shifted(cotangent, "tm", -1)
    future = jnp.concatenate([cotangent, later], axis=0)
    grad_wide = jnp.zeros(clip.shape, jnp.float32)
    for time_lag in range(3):
        grad_wide = grad_wide + flat_dot(
            future[time_lag : time_lag + frame_count], temporal_weight[time_lag].T
        )
    grad_mid = grad_wide.astype(jnp.bfloat16)
    grad_temporal = jnp.stack(
        [
            outer_sum(history[2 - time_lag : 2 - time_lag + frame_count], cotangent)
            for time_lag in range(3)
        ]
    )
    grad_ext = extended(grad_mid, (("height", 1),), 1)
    grad_pad = jnp.pad(grad_ext, ((0, 0), (0, 0), (1, 1), (0, 0)))
    terms = []
    for tap_row in range(3):
        for tap_col in range(3):
            terms.append(
                outer_sum(
                    padded[:, tap_row : tap_row + row_count, tap_col : tap_col + col_count],
                    grad_mid,
                )
            )
    grad_spatial = jnp.stack(terms)
    grad_act = jnp.zeros(clip.shape, jnp.float32)
    for tap_row in range(3):
        for tap_col in range(3):
            grad_act = grad_act + flat_dot(
                grad_pad[
                    :, 2 - tap_row : 2 - tap_row + row_count, 2 - tap_col : 2 - tap_col + col_count
                ],
                spatial_weight[tap_row, tap_col].T,
            )
    unused, pullback = jax.vjp(activate, clip_wide)
    grad_clip = (cotangent.astype(jnp.float32) + pullback(grad_act)[0]).astype(jnp.bfloat16)
    time_shards = lax.axis_size("tm")
    row_shards = lax.axis_size("height")
    grad_scale = 1.0 / math.sqrt(frame_count * time_shards * row_count * row_shards * col_count)
    flat_spatial = (grad_spatial * grad_scale).reshape(-1)
    flat_temporal = (grad_temporal * grad_scale).reshape(-1)
    spatial_part, temporal_part = (
        lax.psum_scatter(flat_spatial, ("tm", "height"), scatter_dimension=0, tiled=True),
        lax.psum_scatter(flat_temporal, ("tm", "height"), scatter_dimension=0, tiled=True),
    )
    return (output, grad_clip, spatial_part, temporal_part)


def solution(mesh):
    return jax.shard_map(
        shards,
        mesh=mesh,
        in_specs=(P("tm", "height", None, None), P("tm", "height", None, None), P(), P()),
        out_specs=(
            P("tm", "height", None, None),
            P("tm", "height", None, None),
            P(("tm", "height")),
            P(("tm", "height")),
        ),
        check_vma=False,
    )
```

profile of v0, /device:TPU:0, one launch (start us, length us, event | category | flops | bytes accessed | tf_op | source)
XLA Modules:
  0.0 200.1 jit_solution(1241580472941981412)
XLA Ops:
  7.2 0.0 copy-start.1
  7.2 0.0 copy-start.3
  7.2 0.0 all-reduce.7.cloned.1.call-start
  7.2 1.4 collective-permute-start.3
  8.7 1.1 fusion.29
  9.8 1.2 fusion.87
  11.0 0.3 fusion.81
  11.3 0.0 copy-start
  11.3 0.3 fusion.7
  11.6 1.4 collective-permute-start.5
  13.0 5.5 %collective-permute-start.4 = (bf16[2,1,64,256]{3,2,1,0:T(8,128)(2,1)S(1)}, bf16[2,1,64,256]{3,2,1,0:T(8,128)(2,1)S(1)}, u32[]{:S(2)}, u32[]{:S(2)}) collective-permute-start(bf16[2,1,64,256]{3,2,1,0:T(8,128)(2,1)S(1)} %get-tuple-element.8), channel_id=1, source_target_pairs={{0,1},{1,2},{2,3},{3,4},{4,5},{5,6},{6,7},{8,9},{9,10},{10,11},{11... | collective-permute-start | bytes 196616 | tf_op jit(solution)/shard_map/ppermute | solution.py:19
  18.6 0.3 collective-permute-done.5
  18.9 1.6 collective-permute-done.4
  20.4 0.1 select_maximum_fusion
  20.6 0.3 fusion.42
  20.8 0.2 fusion.35
  21.1 0.3 convolution_add_fusion.9
  21.4 0.3 convolution_add_fusion.8
  21.6 0.3 convolution_add_fusion.7
  21.9 0.3 convolution_add_fusion.6
  22.2 0.0 copy-start.2
  22.2 0.3 convolution_add_fusion.5
  22.5 0.3 convolution_add_fusion.4
  22.7 0.4 copy-done.2
  23.1 0.5 fusion.30
  23.7 1.0 fusion.28
  24.7 1.3 collective-permute-start.1
  26.0 5.5 %collective-permute-start = (bf16[2,1,64,256]{3,2,1,0:T(8,128)(2,1)S(1)}, bf16[2,1,64,256]{3,2,1,0:T(8,128)(2,1)S(1)}, u32[]{:S(2)}, u32[]{:S(2)}) collective-permute-start(bf16[2,1,64,256]{3,2,1,0:T(8,128)(2,1)S(1)} %get-tuple-element.10), channel_id=1, source_target_pairs={{0,1},{1,2},{2,3},{3,4},{4,5},{5,6},{6,7},{8,9},{9,10},{10,11},{11... | collective-permute-start | bytes 196616 | tf_op jit(solution)/shard_map/ppermute | solution.py:19
  31.5 0.3 collective-permute-done.1
  31.8 1.6 collective-permute-done
  33.4 0.1 select_maximum_fusion.2
  33.5 0.2 fusion.50
  33.7 0.3 fusion.16
  34.0 0.2 fusion.62
  34.2 0.2 convolution_add_fusion.15
  34.5 0.2 convolution_add_fusion.14
  34.7 0.2 convolution_add_fusion.13
  34.9 0.2 convolution_add_fusion.12
  35.2 0.2 convolution_add_fusion.11
  35.4 0.2 convolution_add_fusion.10
  35.6 0.2 fusion.6
  35.9 4.0 %collective-permute-start.2 = (bf16[2,4,64,256]{3,2,1,0:T(8,128)(2,1)S(1)}, bf16[2,4,64,256]{3,2,1,0:T(8,128)(2,1)S(1)}, u32[]{:S(2)}, u32[]{:S(2)}) collective-permute-start(bf16[2,4,64,256]{3,2,1,0:T(8,128)(2,1)S(1)} %fusion.6), channel_id=1, source_target_pairs={{0,8},{8,16},{16,24},{1,9},{9,17},{17,25},{2,10},{10,18},{18,26},{... | collective-permute-start | bytes 786440 | tf_op jit(solution)/shard_map/ppermute | solution.py:31
  39.9 0.3 fusion.9
  40.2 0.3 fusion.15
  40.5 0.3 fusion.14
  40.7 0.3 fusion.13
  41.0 0.3 fusion.12
  41.3 0.3 fusion.11
  41.6 0.3 fusion.8
  41.9 0.3 fusion.10
  42.2 0.2 broadcast_multiply_fusion
  42.3 2.6 %copy.32 = f32[288,2,8,128]{3,1,2,0:T(2,128)} copy(f32[288,2,8,128]{3,2,1,0:T(8,128)S(1)} %bitcast.226) | data formatting | bytes 4718592
  45.0 0.3 convolution_bitcast_fusion.4
  45.2 0.3 convolution_bitcast_fusion.3
  45.5 0.3 convolution_bitcast_fusion
  45.8 0.1 maximum_multiply_fusion
  45.8 1.3 copy.33
  47.1 0.0 all-reduce.7.cloned.1.call-update
  47.2 0.2 fusion.89
  47.4 0.2 fusion.83
  47.6 0.9 fusion.5
  48.6 141.8 %all-reduce.7.cloned.1.call-done = (f32[589824]{0:T(1024)}, f32[196608]{0:T(1024)}) async-done(((f32[589824]{0:T(1024)}, f32[196608]{0:T(1024)}), (f32[589824]{0:T(1024)}, f32[196608]{0:T(1024)})) %all-reduce.7.cloned.1.call-update) | async-done | bytes 3145744
  190.3 1.5 dynamic-slice
  191.9 1.3 dynamic-slice.1
  (9 shorter events, 0.1 us)
Async XLA Ops:
  7.2 4.1 %copy-start.1 = (bf16[2,4,64,256]{3,2,1,0:T(8,128)(2,1)S(1)}, bf16[2,4,64,256]{3,2,1,0:T(8,128)(2,1)}, u32[]{:S(2)}) copy-start(bf16[2,4,64,256]{3,2,1,0:T(8,128)(2,1)} %param.5) | copy-start | bytes 786436
  7.2 3.9 %copy-start.3 = (bf16[3,256,256]{2,1,0:T(8,128)(2,1)S(1)}, bf16[3,256,256]{2,1,0:T(8,128)(2,1)}, u32[]{:S(2)}) copy-start(bf16[3,256,256]{2,1,0:T(8,128)(2,1)} %param.7) | copy-start | bytes 1179652
  7.2 183.2 %all-reduce.7.cloned.1.call-start = ((), (), s32[]{:S(2)}) async-start(), calls=%async_computation | async-start | bytes 6291456
  7.2 3.8 %collective-permute-start.3 = (bf16[2,4,64,256]{3,2,1,0:T(8,128)(2,1)}, bf16[2,4,64,256]{3,2,1,0:T(8,128)(2,1)S(1)}, u32[]{:S(2)}, u32[]{:S(2)}) collective-permute-start(bf16[2,4,64,256]{3,2,1,0:T(8,128)(2,1)} %param.5), channel_id=1, source_target_pairs={{8,0},{16,8},{24,16},{9,1},{17,9},{25,17},{10,2},{18,10},{26,18},{... | collective-permute-start | bytes 786440 | tf_op jit(solution)/shard_map/ppermute | solution.py:31
  11.3 9.3 %copy-start = (bf16[3,3,256,256]{3,2,1,0:T(8,128)(2,1)S(1)}, bf16[3,3,256,256]{3,2,1,0:T(8,128)(2,1)}, u32[]{:S(2)}) copy-start(bf16[3,3,256,256]{3,2,1,0:T(8,128)(2,1)} %param.6) | copy-start | bytes 3538948
  11.6 7.2 %collective-permute-start.5 = (bf16[2,1,64,256]{3,2,1,0:T(8,128)(2,1)S(1)}, bf16[2,1,64,256]{3,2,1,0:T(8,128)(2,1)S(1)}, u32[]{:S(2)}, u32[]{:S(2)}) collective-permute-start(bf16[2,1,64,256]{3,2,1,0:T(8,128)(2,1)S(1)} %get-tuple-element.9), channel_id=1, source_target_pairs={{1,0},{2,1},{3,2},{4,3},{5,4},{6,5},{7,6},{9,8},{10,9},{11,10},{12... | collective-permute-start | bytes 196616 | tf_op jit(solution)/shard_map/ppermute | solution.py:21
  13.0 7.4 %collective-permute-start.4 = (bf16[2,1,64,256]{3,2,1,0:T(8,128)(2,1)S(1)}, bf16[2,1,64,256]{3,2,1,0:T(8,128)(2,1)S(1)}, u32[]{:S(2)}, u32[]{:S(2)}) collective-permute-start(bf16[2,1,64,256]{3,2,1,0:T(8,128)(2,1)S(1)} %get-tuple-element.8), channel_id=1, source_target_pairs={{0,1},{1,2},{2,3},{3,4},{4,5},{5,6},{6,7},{8,9},{9,10},{10,11},{11... | collective-permute-start | bytes 196616 | tf_op jit(solution)/shard_map/ppermute | solution.py:19
  22.2 1.0 copy-start.2
  24.7 7.1 %collective-permute-start.1 = (bf16[2,1,64,256]{3,2,1,0:T(8,128)(2,1)S(1)}, bf16[2,1,64,256]{3,2,1,0:T(8,128)(2,1)S(1)}, u32[]{:S(2)}, u32[]{:S(2)}) collective-permute-start(bf16[2,1,64,256]{3,2,1,0:T(8,128)(2,1)S(1)} %get-tuple-element.11), channel_id=1, source_target_pairs={{1,0},{2,1},{3,2},{4,3},{5,4},{6,5},{7,6},{9,8},{10,9},{11,10},{12... | collective-permute-start | bytes 196616 | tf_op jit(solution)/shard_map/ppermute | solution.py:21
  26.0 7.3 %collective-permute-start = (bf16[2,1,64,256]{3,2,1,0:T(8,128)(2,1)S(1)}, bf16[2,1,64,256]{3,2,1,0:T(8,128)(2,1)S(1)}, u32[]{:S(2)}, u32[]{:S(2)}) collective-permute-start(bf16[2,1,64,256]{3,2,1,0:T(8,128)(2,1)S(1)} %get-tuple-element.10), channel_id=1, source_target_pairs={{0,1},{1,2},{2,3},{3,4},{4,5},{5,6},{6,7},{8,9},{9,10},{10,11},{11... | collective-permute-start | bytes 196616 | tf_op jit(solution)/shard_map/ppermute | solution.py:19
  35.9 9.4 %collective-permute-start.2 = (bf16[2,4,64,256]{3,2,1,0:T(8,128)(2,1)S(1)}, bf16[2,4,64,256]{3,2,1,0:T(8,128)(2,1)S(1)}, u32[]{:S(2)}, u32[]{:S(2)}) collective-permute-start(bf16[2,4,64,256]{3,2,1,0:T(8,128)(2,1)S(1)} %fusion.6), channel_id=1, source_target_pairs={{0,8},{8,16},{16,24},{1,9},{9,17},{17,25},{2,10},{10,18},{18,26},{... | collective-permute-start | bytes 786440 | tf_op jit(solution)/shard_map/ppermute | solution.py:31
Sparse Core Ops, SparseCore 0:
  47.3 143.0 all-reduce.6
where the time goes:
time: 200 us
  waiting for transfers between devices  146 us (73%)
  starting transfers between devices  19.2 us (10%)
  between operations  14.4 us (7%)
  matrix products  11.1 us (6%)
  local copies, waits for them, and re-layouts  7.23 us (4%)
  other arithmetic  2.63 us (1%)
    unnamed x2, waiting for transfers between devices  142 us
    ppermute x2, starting transfers between devices, extended(): lax.ppermute(tail, axis, [(i, (i + 1) % count) for i in range(ends)])  11 us
    dot_general x24, matrix products, flat_dot(): jnp.dot(left.reshape(-1, left.shape[-1]), weight, preferred_element_type=...  7.82 us
    unnamed x12, local copies, waits for them, and re-layouts  7.21 us
    ppermute x2, starting transfers between devices, shifted(): return lax.ppermute(block, axis, route)  5.45 us
  transfers between devices with their start and end apart: 7, of which 5 were waited for; matrix products, arithmetic and copies ran while one was open for 4% of the time, Pallas kernels for 0%

commit v1 on v0

v1 whole, which is shorter than its diff:
```python
import functools
import math

import jax
import jax.numpy as jnp
from jax import lax
from jax.experimental import pallas as pl
from jax.experimental.pallas import tpu as pltpu
from jax.sharding import PartitionSpec as P

EPSILON = 1e-06
MESH = pl.DeviceIdType.MESH
F32 = jnp.float32
BF16 = jnp.bfloat16
NN = (((1,), (0,)), ((), ()))
NT = (((1,), (1,)), ((), ()))
TN = (((0,), (0,)), ((), ()))

SPATIAL_ROWS = 72
TEMPORAL_ROWS = 24
SLICE_ROWS = SPATIAL_ROWS + TEMPORAL_ROWS
HALF = SLICE_ROWS // 2


def dot(left, right, dims=NN):
    return lax.dot_general(left, right, dims, preferred_element_type=F32)


def flat(block):
    return block.reshape(-1, block.shape[-1])


def activate(values):
    scale_inv = lax.rsqrt(jnp.mean(values * values, axis=-1, keepdims=True) + EPSILON)
    normed = values * scale_inv
    return normed / (1.0 + jnp.exp(-normed))


def columns(block):
    wide = block.astype(F32)
    zero = jnp.zeros(wide.shape[:-2] + (1,) + wide.shape[-1:], F32)
    axis = wide.ndim - 2
    count = wide.shape[axis]
    before = jnp.concatenate([zero, lax.slice_in_dim(wide, 0, count - 1, axis=axis)], axis=axis)
    after = jnp.concatenate([lax.slice_in_dim(wide, 1, count, axis=axis), zero], axis=axis)
    return before.astype(BF16), block.astype(BF16), after.astype(BF16)


def body(
    sizes, reduce_inside, clip, cot, sw, tw, out, gclip, gs_out, gt_out,
    clip_halo, cot_next, mid_prev, mid, gm, gm_halo, act3, gm3, gmx, gs, gt, hsend, hrecv, *rest
):
    tm_count, h_count = sizes
    frames, rows, cols, ch = clip.shape
    tm = lax.axis_index("tm")
    hh = lax.axis_index("height")
    cells = rows * cols

    up, down = {"height": hh - 1}, {"height": hh + 1}
    before, after = {"tm": tm - 1}, {"tm": tm + 1}
    has_up, has_down = hh > 0, hh < h_count - 1
    has_before, has_after = tm > 0, tm < tm_count - 1

    barrier = pltpu.get_barrier_semaphore()

    def greet(where, who):
        @pl.when(where)
        def _():
            pl.semaphore_signal(barrier, inc=1, device_id=who, device_id_type=MESH)

    sides = ((has_up, up), (has_down, down), (has_before, before), (has_after, after))
    for where, who in sides:
        greet(where, who)
    if reduce_inside:
        core, xx, yy, zz = lax.rem(tm, 2), tm // 2, lax.rem(hh, 2), hh // 2
        by_core = {"tm": xx * 2 + 1 - core}
        by_x = {"tm": (1 - xx) * 2 + core}
        by_y = {"height": zz * 2 + 1 - yy}
        by_z = [{"height": lax.rem(zz + off, 4) * 2 + yy} for off in (1, 2, 3)]
        for who in [by_core, by_x, by_y] + by_z:
            pl.semaphore_signal(barrier, inc=1, device_id=who, device_id_type=MESH)

    greeted = 6 if reduce_inside else 0
    for where, who in sides:
        greeted = greeted + where.astype(jnp.int32)
    pl.semaphore_wait(barrier, greeted)

    def copy(src, dst, slot, who):
        return pltpu.make_async_remote_copy(
            src_ref=src, dst_ref=dst, send_sem=hsend.at[slot], recv_sem=hrecv.at[slot],
            device_id=who, device_id_type=MESH,
        )

    def exchange(slot, src_first, src_last, dst, send_up, send_down):
        return (
            (copy(src_first, dst.at[1], slot, up), has_up, has_down),
            (copy(src_last, dst.at[0], slot + 1, down), has_down, has_up),
        )

    def start(c):
        @pl.when(c[1])
        def _():
            c[0].start()

    def wait_recv(c, target):
        @pl.when(c[2])
        def _():
            c[0].wait_recv()

        @pl.when(jnp.logical_not(c[2]))
        def _():
            target[...] = jnp.zeros(target.shape, target.dtype)

    def wait_send(c):
        @pl.when(c[1])
        def _():
            c[0].wait_send()

    cot_copy = (copy(cot, cot_next, 0, before), has_before, has_after)
    clip_up, clip_down = exchange(1, clip.at[:, 0], clip.at[:, rows - 1], clip_halo, up, down)
    start(clip_up)
    start(clip_down)
    start(cot_copy)

    zero_edge = jnp.zeros((frames, 1, cols, ch), BF16)
    for r in range(3):
        lanes = pl.ds(r * ch, ch)
        for row in range(rows + 2):
            if not r <= row < r + rows:
                gmx[:, row : row + 1, :, lanes] = zero_edge

    def put_act(f, row, values):
        act = activate(values.astype(F32))
        for q, part in enumerate(columns(act)):
            act3[f, row, :, pl.ds(q * ch, ch)] = part

    for f in range(frames):
        for row in range(rows):
            put_act(f, row + 1, clip[f, row])
    wait_recv(clip_up, clip_halo.at[1])
    wait_recv(clip_down, clip_halo.at[0])
    for f in range(frames):
        put_act(f, 0, clip_halo[0, f])
        put_act(f, rows + 1, clip_halo[1, f])

    for f in range(frames):
        total = None
        for r in range(3):
            term = dot(flat(act3[f, r : r + rows]), flat(sw[r]))
            total = term if total is None else total + term
        mid[f] = total.astype(BF16).reshape(rows, cols, ch)
    mid_copy = (copy(mid, mid_prev, 3, after), has_after, has_before)
    start(mid_copy)

    wait_recv(cot_copy, cot_next)

    def future(t):
        return cot[t] if t < frames else cot_next[t - frames]

    for f in range(frames):
        total = None
        for k in range(3):
            term = dot(flat(future(f + k)), tw[k], NT)
            total = term if total is None else total + term
        value = total.astype(BF16).reshape(rows, cols, ch)
        gm[f] = value
        for r in range(3):
            gmx[f, r : r + rows, :, pl.ds(r * ch, ch)] = value
    gm_up, gm_down = exchange(4, gm.at[:, 0], gm.at[:, rows - 1], gm_halo, up, down)
    start(gm_up)
    start(gm_down)

    wide = frames * (rows + 2) * cols
    for q in range(3):
        left = act3[:, :, :, pl.ds(q * ch, ch)].reshape(wide, ch)
        for r in range(3):
            right = gmx[:, :, :, pl.ds(r * ch, ch)].reshape(wide, ch)
            gs[pl.ds((r * 3 + q) * ch, ch), :] = dot(left, right, TN)

    wait_recv(mid_copy, mid_prev)

    def history(t):
        return mid[t] if t >= 0 else mid_prev[frames + t]

    for k in range(3):
        total = None
        for f in range(frames):
            term = dot(flat(history(f - k)), flat(cot[f]), TN)
            total = term if total is None else total + term
        gt[pl.ds(k * ch, ch), :] = total

    def do_output(f):
        total = flat(clip[f]).astype(F32)
        for k in range(3):
            total = total + dot(flat(history(f - k)), tw[k])
        out[f] = total.astype(BF16).reshape(rows, cols, ch)

    def do_gm3():
        wait_recv(gm_up, gm_halo.at[1])
        wait_recv(gm_down, gm_halo.at[0])
        for f in range(frames):
            for row in range(rows + 2):
                if row == 0:
                    value = gm_halo[0, f]
                elif row == rows + 1:
                    value = gm_halo[1, f]
                else:
                    value = gm[f, row - 1]
                shifts = columns(value)
                for q in range(3):
                    gm3[f, row, :, pl.ds(q * ch, ch)] = shifts[2 - q]

    def do_grad_clip(f):
        total = None
        for r in range(3):
            for q in range(3):
                left = flat(gm3[f, 2 - r : 2 - r + rows, :, pl.ds(q * ch, ch)])
                term = dot(left, sw[r, q], NT)
                total = term if total is None else total + term
        values = flat(clip[f]).astype(F32)
        scale_inv = lax.rsqrt(jnp.mean(values * values, axis=-1, keepdims=True) + EPSILON)
        normed = values * scale_inv
        gate = 1.0 / (1.0 + jnp.exp(-normed))
        inner = total * (gate * (1.0 + normed * (1.0 - gate)))
        slope = scale_inv * (inner - normed * jnp.mean(inner * normed, axis=-1, keepdims=True))
        gclip[f] = (flat(cot[f]).astype(F32) + slope).astype(BF16).reshape(rows, cols, ch)

    scale = 1.0 / math.sqrt(frames * tm_count * rows * h_count * cols)

    if not reduce_inside:
        for f in range(frames):
            do_output(f)
        do_gm3()
        for f in range(frames):
            do_grad_clip(f)
        gs_out[...] = gs[...] * scale
        gt_out[...] = gt[...] * scale
    else:
        (send0, recv0, part, send_a1, recv_a1, send_b1, recv_b1, send_a2, recv_a2, send_b2, recv_b2,
         send_z, recv_z, total_z, rsend, rrecv) = rest

        def rcopy(src, dst, slot, who):
            return pltpu.make_async_remote_copy(
                src_ref=src, dst_ref=dst, send_sem=rsend.at[slot], recv_sem=rrecv.at[slot],
                device_id=who, device_id_type=MESH,
            )

        def slice_of(d):
            top = gs[pl.ds(pl.multiple_of(d * SPATIAL_ROWS, 8), SPATIAL_ROWS), :]
            low = gt[pl.ds(pl.multiple_of(d * TEMPORAL_ROWS, 8), TEMPORAL_ROWS), :]
            return jnp.concatenate([top, low], axis=0)

        def each(count):
            def run(step):
                lax.fori_loop(0, count, lambda j, carry: (step(j), carry)[1], 0)
            return run

        @each(16)
        def _(j):
            send0[j] = slice_of(((j // 8) * 2 + 1 - core) * 8 + lax.rem(j, 8)).astype(BF16)

        c0 = rcopy(send0, recv0, 0, by_core)
        c0.start()
        do_output(0)
        do_gm3()
        c0.wait()

        @each(16)
        def _(j):
            own = slice_of(((j // 8) * 2 + core) * 8 + lax.rem(j, 8))
            part[j] = own + recv0[j].astype(F32)

        @each(8)
        def _(j):
            send_a1[j] = part[(1 - xx) * 8 + j, :HALF].astype(BF16)
            send_b1[j] = part[j * 2 + 1 - yy, HALF:].astype(BF16)

        ca = rcopy(send_a1, recv_a1, 1, by_x)
        cb = rcopy(send_b1, recv_b1, 2, by_y)
        ca.start()
        cb.start()
        do_grad_clip(0)
        ca.wait()
        cb.wait()

        @each(8)
        def _(j):
            here = xx * 8 + j
            part[here, :HALF] = part[here, :HALF] + recv_a1[j].astype(F32)
            there = j * 2 + yy
            part[there, HALF:] = part[there, HALF:] + recv_b1[j].astype(F32)

        @each(4)
        def _(j):
            send_a2[j] = part[xx * 8 + j * 2 + 1 - yy, :HALF].astype(BF16)
            send_b2[j] = part[(1 - xx) * 8 + j * 2 + yy, HALF:].astype(BF16)

        ca2 = rcopy(send_a2, recv_a2, 3, by_y)
        cb2 = rcopy(send_b2, recv_b2, 4, by_x)
        ca2.start()
        cb2.start()
        do_output(1)
        ca2.wait()
        cb2.wait()

        @each(4)
        def _(j):
            place = xx * 8 + j * 2 + yy
            value = part[place] + jnp.concatenate(
                [recv_a2[j].astype(F32), recv_b2[j].astype(F32)], axis=0
            )
            total_z[j] = value
            send_z[j] = value.astype(BF16)

        cz = [
            rcopy(send_z.at[lax.rem(zz + off, 4)], recv_z.at[off - 1], 4 + off, by_z[off - 1])
            for off in (1, 2, 3)
        ]
        for c in cz:
            c.start()
        do_grad_clip(1)
        for c in cz:
            c.wait()
        value = total_z[zz]
        for off in range(3):
            value = value + recv_z[off].astype(F32)
        value = value * scale
        gs_out[...] = value[:SPATIAL_ROWS]
        gt_out[...] = value[SPATIAL_ROWS:]

    for c in (clip_up, clip_down, cot_copy, mid_copy, gm_up, gm_down):
        wait_send(c)


def shards(sizes, clip, cot, sw, tw):
    tm_count, h_count = sizes
    frames, rows, cols, ch = clip.shape
    inside = sizes == (4, 8) and ch == 256 and frames == 2
    wide = (frames, rows + 2, cols, 3 * ch)
    edge = (2, frames, cols, ch)
    vmem = pl.BlockSpec(memory_space=pltpu.VMEM)
    scratch = [
        pltpu.VMEM(edge, BF16),
        pltpu.VMEM(clip.shape, BF16),
        pltpu.VMEM(clip.shape, BF16),
        pltpu.VMEM(clip.shape, BF16),
        pltpu.VMEM(clip.shape, BF16),
        pltpu.VMEM(edge, BF16),
        pltpu.VMEM(wide, BF16),
        pltpu.VMEM(wide, BF16),
        pltpu.VMEM(wide, BF16),
        pltpu.VMEM((9 * ch, ch), F32),
        pltpu.VMEM((3 * ch, ch), F32),
        pltpu.SemaphoreType.DMA((6,)),
        pltpu.SemaphoreType.DMA((6,)),
    ]
    gs_shape, gt_shape = (9 * ch, ch), (3 * ch, ch)
    if inside:
        gs_shape, gt_shape = (SPATIAL_ROWS, ch), (TEMPORAL_ROWS, ch)
        scratch += [
            pltpu.VMEM((16, SLICE_ROWS, ch), BF16),
            pltpu.VMEM((16, SLICE_ROWS, ch), BF16),
            pltpu.VMEM((16, SLICE_ROWS, ch), F32),
        ]
        scratch += [pltpu.VMEM((8, HALF, ch), BF16)] * 4
        scratch += [pltpu.VMEM((4, HALF, ch), BF16)] * 4
        scratch += [
            pltpu.VMEM((4, SLICE_ROWS, ch), BF16),
            pltpu.VMEM((3, SLICE_ROWS, ch), BF16),
            pltpu.VMEM((4, SLICE_ROWS, ch), F32),
            pltpu.SemaphoreType.DMA((8,)),
            pltpu.SemaphoreType.DMA((8,)),
        ]
    out, gclip, gs, gt = pl.pallas_call(
        functools.partial(body, sizes, inside),
        out_shape=(
            jax.ShapeDtypeStruct(clip.shape, BF16),
            jax.ShapeDtypeStruct(clip.shape, BF16),
            jax.ShapeDtypeStruct(gs_shape, F32),
            jax.ShapeDtypeStruct(gt_shape, F32),
        ),
        in_specs=[vmem] * 4,
        out_specs=(vmem,) * 4,
        scratch_shapes=scratch,
        compiler_params=pltpu.CompilerParams(
            collective_id=0, has_side_effects=True, vmem_limit_bytes=48 * 1024 * 1024
        ),
        name="section",
    )(clip, cot, sw, tw)
    gs, gt = gs.reshape(-1), gt.reshape(-1)
    if not inside:
        gs, gt = (
            lax.psum_scatter(gs, ("tm", "height"), scatter_dimension=0, tiled=True),
            lax.psum_scatter(gt, ("tm", "height"), scatter_dimension=0, tiled=True),
        )
    return out, gclip, gs, gt


def solution(mesh):
    sizes = (mesh.shape["tm"], mesh.shape["height"])
    return jax.shard_map(
        functools.partial(shards, sizes),
        mesh=mesh,
        in_specs=(P("tm", "height", None, None), P("tm", "height", None, None), P(), P()),
        out_specs=(
            P("tm", "height", None, None),
            P("tm", "height", None, None),
            P(("tm", "height")),
            P(("tm", "height")),
        ),
        check_vma=False,
    )
```

time: 200 us -> 40.3 us (0.20)
  waiting for transfers between devices: 146 us -> 0 us
  Pallas kernels: 0 us -> 32.6 us
  starting transfers between devices: 19.2 us -> 0 us
  between operations: 14.4 us -> 0.65 us
  matrix products: 11.1 us -> 0 us
  other arithmetic: 2.63 us -> 0 us
    unnamed x2 -> x0, waiting for transfers between devices: 142 us -> none
    pallas_call x0 -> x1, Pallas kernels: none -> 32.6 us  [shards(): pl.pallas_call(functools.partial(body, sizes, inside), out_shape=(jax.Sha...]
    ppermute x6 -> x0, starting transfers between devices: 19.1 us -> none  [the longest x2 11 us: extended(): lax.ppermute(tail, axis, [(i, (i + 1) % count) for i in range(ends)])]
    dot_general x36 -> x0, matrix products: 11.1 us -> none  [the longest x24 7.82 us: flat_dot(): jnp.dot(left.reshape(-1, left.shape[-1]), weight, preferred_element_type=...]
    ppermute x6 -> x0, waiting for transfers between devices: 3.76 us -> none  [the longest x2 3.16 us: extended(): lax.ppermute(tail, axis, [(i, (i + 1) % count) for i in range(ends)])]
  transfers between devices with their start and end apart: 7 -> 0, of which waited for: 5 -> 0; matrix products, arithmetic and copies ran while one was open for 4% -> 0% of each run, Pallas kernels for 0% -> 0%
where the time goes in v1:
time: 40.3 us; the launch traced here: 40.1 us
  Pallas kernels  32.6 us (81%)
  local copies, waits for them, and re-layouts  6.85 us (17%)
  between operations  0.65 us (2%)
    pallas_call x1, Pallas kernels, shards(): pl.pallas_call(functools.partial(body, sizes, inside), out_shape=(jax.Sha...  32.6 us
    unnamed x12, local copies, waits for them, and re-layouts  6.85 us

profile of v1, /device:TPU:0, one launch (start us, length us, event | category | flops | bytes accessed | tf_op | source)
XLA Modules:
  0.0 40.1 jit_solution(3039857649104122516)
XLA Ops:
  0.6 0.0 copy-start
  0.6 1.3 %copy-done = bf16[3,3,256,256]{3,2,1,0:T(8,128)(2,1)S(1)} copy-done((bf16[3,3,256,256]{3,2,1,0:T(8,128)(2,1)S(1)}, bf16[3,3,256,256]{3,2,1,0:T(8,128)(2,1)}, u32[]{:S(2)}) %copy-start) | copy-done | bytes 1179672
  1.9 0.0 copy-start.1
  1.9 1.0 %copy-done.1 = bf16[3,256,256]{2,1,0:T(8,128)(2,1)S(1)} copy-done((bf16[3,256,256]{2,1,0:T(8,128)(2,1)S(1)}, bf16[3,256,256]{2,1,0:T(8,128)(2,1)}, u32[]{:S(2)}) %copy-start.1) | copy-done | bytes 393240
  2.9 0.0 copy-start.2
  2.9 0.9 %copy-done.2 = bf16[2,4,64,256]{3,2,1,0:T(8,128)(2,1)S(1)} copy-done((bf16[2,4,64,256]{3,2,1,0:T(8,128)(2,1)S(1)}, bf16[2,4,64,256]{3,2,1,0:T(8,128)(2,1)}, u32[]{:S(2)}) %copy-start.2) | copy-done | bytes 262168
  3.9 0.0 copy-start.3
  3.9 0.9 %copy-done.3 = bf16[2,4,64,256]{3,2,1,0:T(8,128)(2,1)S(1)} copy-done((bf16[2,4,64,256]{3,2,1,0:T(8,128)(2,1)S(1)}, bf16[2,4,64,256]{3,2,1,0:T(8,128)(2,1)}, u32[]{:S(2)}) %copy-start.3) | copy-done | bytes 262168
  4.8 32.6 %section.1 = (bf16[2,4,64,256]{3,2,1,0:T(8,128)(2,1)S(1)}, bf16[2,4,64,256]{3,2,1,0:T(8,128)(2,1)S(1)}, f32[72,256]{1,0:T(8,128)S(1)}, f32[24,256]{1,0:T(8,128)S(1)}) custom-call(bf16[2,4,64,256]{3,2,1,0:T(8,128)(2,1)S(1)} %copy-done.2, bf16[2,4,64,256]{3,2,1,0:T(8,128)(2,1)S(1)} %copy-done.3, bf16[3,3,256,256]{3,2,1,0:T(8,128)(2,1)S(1)} %copy-done, ...), custom_call_target="tpu_custom_call" | custom-call | tf_op jit(solution)/shard_map/section/pallas_call | solution.py:374
  37.4 0.6 %copy.9 = f32[3,2,8,128]{3,1,2,0:T(2,128)} copy(f32[3,2,8,128]{3,2,1,0:T(8,128)S(1)} %bitcast.5) | data formatting | bytes 49152
  38.0 0.7 %copy.8 = f32[9,2,8,128]{3,1,2,0:T(2,128)} copy(f32[9,2,8,128]{3,2,1,0:T(8,128)S(1)} %bitcast.4) | data formatting | bytes 147456
  38.7 0.7 %copy.12 = bf16[2,4,64,256]{3,2,1,0:T(8,128)(2,1)} copy(bf16[2,4,64,256]{3,2,1,0:T(8,128)(2,1)S(1)} %get-tuple-element.16) | data formatting | bytes 524288
  39.4 0.7 %copy.13 = bf16[2,4,64,256]{3,2,1,0:T(8,128)(2,1)} copy(bf16[2,4,64,256]{3,2,1,0:T(8,128)(2,1)S(1)} %get-tuple-element.17) | data formatting | bytes 524288
Async XLA Ops:
  0.6 1.3 %copy-start = (bf16[3,3,256,256]{3,2,1,0:T(8,128)(2,1)S(1)}, bf16[3,3,256,256]{3,2,1,0:T(8,128)(2,1)}, u32[]{:S(2)}) copy-start(bf16[3,3,256,256]{3,2,1,0:T(8,128)(2,1)} %sw.1) | copy-start | bytes 3538948
  1.9 1.0 %copy-start.1 = (bf16[3,256,256]{2,1,0:T(8,128)(2,1)S(1)}, bf16[3,256,256]{2,1,0:T(8,128)(2,1)}, u32[]{:S(2)}) copy-start(bf16[3,256,256]{2,1,0:T(8,128)(2,1)} %tw.1) | copy-start | bytes 1179652
  2.9 0.9 %copy-start.2 = (bf16[2,4,64,256]{3,2,1,0:T(8,128)(2,1)S(1)}, bf16[2,4,64,256]{3,2,1,0:T(8,128)(2,1)}, u32[]{:S(2)}) copy-start(bf16[2,4,64,256]{3,2,1,0:T(8,128)(2,1)} %clip.1) | copy-start | bytes 786436
  3.9 0.9 %copy-start.3 = (bf16[2,4,64,256]{3,2,1,0:T(8,128)(2,1)S(1)}, bf16[2,4,64,256]{3,2,1,0:T(8,128)(2,1)}, u32[]{:S(2)}) copy-start(bf16[2,4,64,256]{3,2,1,0:T(8,128)(2,1)} %cot.1) | copy-start | bytes 786436

commit v2 on v1

v2 whole, which is shorter than its diff:
```python
import functools
import math

import jax
import jax.numpy as jnp
from jax import lax
from jax.experimental import pallas as pl
from jax.experimental.pallas import tpu as pltpu
from jax.sharding import PartitionSpec as P

EPSILON = 1e-06
MESH = pl.DeviceIdType.MESH
F32 = jnp.float32
BF16 = jnp.bfloat16
NN = (((1,), (0,)), ((), ()))
NT = (((1,), (1,)), ((), ()))
TN = (((0,), (0,)), ((), ()))

SPATIAL_ROWS = 72
TEMPORAL_ROWS = 24
LANES = 128
CHUNKS = (("spatial", 0, 32, 32), ("spatial", 64, 32, 48), ("temporal", 0, 32, 16))


def dot(left, right, dims=NN):
    return lax.dot_general(left, right, dims, preferred_element_type=F32)


def flat(block):
    return block.reshape(-1, block.shape[-1])


def activate(values):
    scale_inv = lax.rsqrt(jnp.mean(values * values, axis=-1, keepdims=True) + EPSILON)
    normed = values * scale_inv
    return normed / (1.0 + jnp.exp(-normed))


def columns(block):
    wide = block.astype(F32)
    zero = jnp.zeros(wide.shape[:-2] + (1,) + wide.shape[-1:], F32)
    axis = wide.ndim - 2
    count = wide.shape[axis]
    before = jnp.concatenate([zero, lax.slice_in_dim(wide, 0, count - 1, axis=axis)], axis=axis)
    after = jnp.concatenate([lax.slice_in_dim(wide, 1, count, axis=axis), zero], axis=axis)
    return before.astype(BF16), block.astype(BF16), after.astype(BF16)


def body(
    sizes, reduce_inside, clip_hbm, cot_hbm, sw_hbm, tw_hbm, out_hbm, gclip_hbm, gs_out, gt_out,
    clip, cot, sw, tw, out, gclip, in_sem, out_sem,
    clip_halo, cot_next, mid_prev, mid, gm, gm_halo, act3, gm3, act_t, gs, gt, hsend, hrecv, *rest
):
    tm_count, h_count = sizes
    frames, rows, cols, ch = clip.shape
    tm = lax.axis_index("tm")
    hh = lax.axis_index("height")
    cells = rows * cols

    loads = [
        pltpu.make_async_copy(src, dst, in_sem.at[i])
        for i, (src, dst) in enumerate(
            ((clip_hbm, clip), (cot_hbm, cot), (sw_hbm, sw), (tw_hbm, tw))
        )
    ]
    for load in loads:
        load.start()

    up, down = {"height": hh - 1}, {"height": hh + 1}
    before, after = {"tm": tm - 1}, {"tm": tm + 1}
    has_up, has_down = hh > 0, hh < h_count - 1
    has_before, has_after = tm > 0, tm < tm_count - 1

    barrier = pltpu.get_barrier_semaphore()

    def greet(where, who):
        @pl.when(where)
        def _():
            pl.semaphore_signal(barrier, inc=1, device_id=who, device_id_type=MESH)

    sides = ((has_up, up), (has_down, down), (has_before, before), (has_after, after))
    for where, who in sides:
        greet(where, who)
    if reduce_inside:
        core, xx, yy, zz = lax.rem(tm, 2), tm // 2, lax.rem(hh, 2), hh // 2
        by_core = {"tm": xx * 2 + 1 - core}
        by_x = {"tm": (1 - xx) * 2 + core}
        by_y = {"height": zz * 2 + 1 - yy}
        by_z = [{"height": lax.rem(zz + off, 4) * 2 + yy} for off in (1, 2, 3)]
        for who in [by_core, by_x, by_y] + by_z:
            pl.semaphore_signal(barrier, inc=1, device_id=who, device_id_type=MESH)

    greeted = 6 if reduce_inside else 0
    for where, who in sides:
        greeted = greeted + where.astype(jnp.int32)
    pl.semaphore_wait(barrier, greeted)

    def copy(src, dst, slot, who):
        return pltpu.make_async_remote_copy(
            src_ref=src, dst_ref=dst, send_sem=hsend.at[slot], recv_sem=hrecv.at[slot],
            device_id=who, device_id_type=MESH,
        )

    def exchange(slot, src_first, src_last, dst, send_up, send_down):
        return (
            (copy(src_first, dst.at[1], slot, up), has_up, has_down),
            (copy(src_last, dst.at[0], slot + 1, down), has_down, has_up),
        )

    def start(c):
        @pl.when(c[1])
        def _():
            c[0].start()

    def wait_recv(c, target):
        @pl.when(c[2])
        def _():
            c[0].wait_recv()

        @pl.when(jnp.logical_not(c[2]))
        def _():
            target[...] = jnp.zeros(target.shape, target.dtype)

    def wait_send(c):
        @pl.when(c[1])
        def _():
            c[0].wait_send()

    cot_copy = (copy(cot_hbm, cot_next, 0, before), has_before, has_after)
    clip_up, clip_down = exchange(1, clip_hbm.at[:, 0], clip_hbm.at[:, rows - 1], clip_halo, up, down)
    start(clip_up)
    start(clip_down)
    start(cot_copy)

    loads[0].wait()

    def put_act(f, row, values):
        act = activate(values.astype(F32))
        for q, part in enumerate(columns(act)):
            act3[f, row, :, pl.ds(q * ch, ch)] = part

    for f in range(frames):
        for row in range(rows):
            put_act(f, row + 1, clip[f, row])
    wait_recv(clip_up, clip_halo.at[1])
    wait_recv(clip_down, clip_halo.at[0])
    for f in range(frames):
        put_act(f, 0, clip_halo[0, f])
        put_act(f, rows + 1, clip_halo[1, f])

    loads[2].wait()
    for f in range(frames):
        total = None
        for r in range(3):
            term = dot(flat(act3[f, r : r + rows]), flat(sw[r]))
            total = term if total is None else total + term
        mid[f] = total.astype(BF16).reshape(rows, cols, ch)
    mid_copy = (copy(mid, mid_prev, 3, after), has_after, has_before)
    start(mid_copy)

    for r in range(3):
        for f in range(frames):
            act_t[r, :, pl.ds(f * cells, cells)] = flat(
                act3[f, r : r + rows, :, pl.ds(ch, ch)]
            ).T

    loads[1].wait()
    loads[3].wait()
    wait_recv(cot_copy, cot_next)

    def put_gm(f, row, values):
        shifts = columns(values)
        for q in range(3):
            gm3[f, row, :, pl.ds(q * ch, ch)] = shifts[2 - q]

    def future(t):
        return cot[t] if t < frames else cot_next[t - frames]

    for f in range(frames):
        total = None
        for k in range(3):
            term = dot(flat(future(f + k)), tw[k], NT)
            total = term if total is None else total + term
        value = total.astype(BF16).reshape(rows, cols, ch)
        gm[f] = value
        for row in range(rows):
            put_gm(f, row + 1, value[row])
    gm_up, gm_down = exchange(4, gm.at[:, 0], gm.at[:, rows - 1], gm_halo, up, down)
    start(gm_up)
    start(gm_down)

    for r in range(3):
        total = None
        for f in range(frames):
            term = dot(
                act_t[r, :, pl.ds(f * cells, cells)], flat(gm3[f, 1 : 1 + rows])
            )
            total = term if total is None else total + term
        for q in range(3):
            gs[pl.ds((r * 3 + q) * ch, ch), :] = total[:, q * ch : (q + 1) * ch]

    def history(t):
        return mid[t] if t >= 0 else mid_prev[frames + t]

    def do_temporal():
        wait_recv(mid_copy, mid_prev)
        turned = {t: flat(history(t)).T for t in range(-2, frames)}
        for k in range(3):
            total = None
            for f in range(frames):
                term = dot(turned[f - k], flat(cot[f]))
                total = term if total is None else total + term
            gt[pl.ds(k * ch, ch), :] = total

    stores = []

    def store(src, dst, f, slot):
        c = pltpu.make_async_copy(src.at[f], dst.at[f], out_sem.at[slot])
        c.start()
        stores.append(c)

    def do_output(f):
        total = flat(clip[f]).astype(F32)
        for k in range(3):
            total = total + dot(flat(history(f - k)), tw[k])
        out[f] = total.astype(BF16).reshape(rows, cols, ch)
        store(out, out_hbm, f, f)

    def do_gm_halo():
        wait_recv(gm_up, gm_halo.at[1])
        wait_recv(gm_down, gm_halo.at[0])
        for f in range(frames):
            put_gm(f, 0, gm_halo[0, f])
            put_gm(f, rows + 1, gm_halo[1, f])

    def do_grad_clip(f):
        total = None
        for r in range(3):
            for q in range(3):
                left = flat(gm3[f, 2 - r : 2 - r + rows, :, pl.ds(q * ch, ch)])
                term = dot(left, sw[r, q], NT)
                total = term if total is None else total + term
        values = flat(clip[f]).astype(F32)
        scale_inv = lax.rsqrt(jnp.mean(values * values, axis=-1, keepdims=True) + EPSILON)
        normed = values * scale_inv
        gate = 1.0 / (1.0 + jnp.exp(-normed))
        inner = total * (gate * (1.0 + normed * (1.0 - gate)))
        slope = scale_inv * (inner - normed * jnp.mean(inner * normed, axis=-1, keepdims=True))
        gclip[f] = (flat(cot[f]).astype(F32) + slope).astype(BF16).reshape(rows, cols, ch)
        store(gclip, gclip_hbm, f, frames + f)

    scale = 1.0 / math.sqrt(frames * tm_count * rows * h_count * cols)

    if not reduce_inside:
        do_temporal()
        for f in range(frames):
            do_output(f)
        do_gm_halo()
        for f in range(frames):
            do_grad_clip(f)
        gs_out[...] = gs[...] * scale
        gt_out[...] = gt[...] * scale
    else:
        rsend, rrecv = rest[-2:]
        bufs = [rest[11 * i : 11 * i + 11] for i in range(len(CHUNKS))]

        def rcopy(src, dst, slot, who):
            return pltpu.make_async_remote_copy(
                src_ref=src, dst_ref=dst, send_sem=rsend.at[slot], recv_sem=rrecv.at[slot],
                device_id=who, device_id_type=MESH,
            )

        def piece(chunk, d):
            kind, first, a, b = chunk
            ref, count = (gs, SPATIAL_ROWS) if kind == "spatial" else (gt, TEMPORAL_ROWS)
            block = ref[pl.ds(pl.multiple_of(d * count, 8), count), :]
            both = jnp.concatenate([block[:, :LANES], block[:, LANES:]], axis=0)
            return both[first : first + a + b]

        def each(count):
            def run(step):
                def four(j, carry):
                    for i in range(4):
                        step(j * 4 + i)
                    return carry

                lax.fori_loop(0, count // 4, four, 0)

            return run

        def owner(j, which):
            return ((j // 8) * 2 + which) * 8 + lax.rem(j, 8)

        def stage_core(i):
            send0, recv0 = bufs[i][:2]

            @each(16)
            def _(j):
                send0[j] = piece(CHUNKS[i], owner(j, 1 - core)).astype(BF16)

            c = rcopy(send0, recv0, 8 * i, by_core)
            c.start()
            return [c]

        def stage_one(i):
            a = CHUNKS[i][2]
            send0, recv0, part, send_a, recv_a, send_b, recv_b = bufs[i][:7]

            @each(16)
            def _(j):
                part[j] = piece(CHUNKS[i], owner(j, core)) + recv0[j].astype(F32)

            @each(8)
            def _(j):
                send_a[j] = part[(1 - xx) * 8 + j, :a].astype(BF16)
                send_b[j] = part[j * 2 + 1 - yy, a:].astype(BF16)

            cs = [
                rcopy(send_a, recv_a, 8 * i + 1, by_x),
                rcopy(send_b, recv_b, 8 * i + 2, by_y),
            ]
            for c in cs:
                c.start()
            return cs

        def stage_two(i):
            a = CHUNKS[i][2]
            part, _, recv_a, _, recv_b, send_a2, recv_a2, send_b2, recv_b2 = bufs[i][2:11]

            @each(4)
            def _(j):
                away = j * 2 + 1 - yy
                send_a2[j] = (part[xx * 8 + away, :a] + recv_a[away].astype(F32)).astype(BF16)
                far = (1 - xx) * 4 + j
                send_b2[j] = (part[far * 2 + yy, a:] + recv_b[far].astype(F32)).astype(BF16)

            cs = [
                rcopy(send_a2, recv_a2, 8 * i + 3, by_y),
                rcopy(send_b2, recv_b2, 8 * i + 4, by_x),
            ]
            for c in cs:
                c.start()
            return cs

        z_bufs = rest[11 * len(CHUNKS) : -2]

        def stage_z(i):
            a = CHUNKS[i][2]
            part, _, recv_a, _, recv_b, _, recv_a2, _, recv_b2 = bufs[i][2:11]
            total_z, send_z, recv_z = z_bufs[3 * i : 3 * i + 3]

            @each(4)
            def _(j):
                near = j * 2 + yy
                first = part[xx * 8 + near, :a] + recv_a[near].astype(F32) + recv_a2[j].astype(F32)
                last = (
                    part[xx * 8 + near, a:] + recv_b[xx * 4 + j].astype(F32) + recv_b2[j].astype(F32)
                )
                value = jnp.concatenate([first, last], axis=0)
                total_z[j] = value
                send_z[j] = value.astype(BF16)

            cs = [
                rcopy(
                    send_z.at[lax.rem(zz + off, 4)], recv_z.at[off - 1], 8 * i + 4 + off, by_z[off - 1]
                )
                for off in (1, 2, 3)
            ]
            for c in cs:
                c.start()
            return cs

        def final(i):
            total_z, _, recv_z = z_bufs[3 * i : 3 * i + 3]
            value = total_z[zz]
            for off in range(3):
                value = value + recv_z[off].astype(F32)
            return value * scale

        def finish(copies):
            for c in copies:
                c.wait()

        def place(ref, value, count):
            ref[pl.ds(0, count, stride=2), :] = value[:count]
            ref[pl.ds(1, count, stride=2), :] = value[count:]

        spatial = (0, 1)
        flight = {i: stage_core(i) for i in spatial}
        do_temporal()
        flight[2] = stage_core(2)

        def advance(stage):
            for i in range(len(CHUNKS)):
                finish(flight[i])
                flight[i] = stage(i)

        advance(stage_one)
        do_output(0)
        do_output(1)
        do_gm_halo()
        advance(stage_two)
        do_grad_clip(0)
        advance(stage_z)
        do_grad_clip(1)
        done = []
        for i in range(len(CHUNKS)):
            finish(flight[i])
            done.append(final(i))
        place(gs_out, jnp.concatenate(done[:2], axis=0), SPATIAL_ROWS)
        place(gt_out, done[2], TEMPORAL_ROWS)

    for c in (clip_up, clip_down, cot_copy, mid_copy, gm_up, gm_down):
        wait_send(c)
    for c in stores:
        c.wait()


def shards(sizes, clip, cot, sw, tw):
    tm_count, h_count = sizes
    frames, rows, cols, ch = clip.shape
    inside = sizes == (4, 8) and ch == 256 and frames == 2
    wide = (frames, rows + 2, cols, 3 * ch)
    edge = (2, frames, cols, ch)
    vmem = pl.BlockSpec(memory_space=pltpu.VMEM)
    scratch = [pltpu.VMEM(x.shape, x.dtype) for x in (clip, cot, sw, tw, clip, clip)]
    scratch += [
        pltpu.SemaphoreType.DMA((4,)),
        pltpu.SemaphoreType.DMA((2 * frames,)),
        pltpu.VMEM(edge, BF16),
        pltpu.VMEM(clip.shape, BF16),
        pltpu.VMEM(clip.shape, BF16),
        pltpu.VMEM(clip.shape, BF16),
        pltpu.VMEM(clip.shape, BF16),
        pltpu.VMEM(edge, BF16),
        pltpu.VMEM(wide, BF16),
        pltpu.VMEM(wide, BF16),
        pltpu.VMEM((3, ch, frames * rows * cols), BF16),
        pltpu.VMEM((9 * ch, ch), F32),
        pltpu.VMEM((3 * ch, ch), F32),
        pltpu.SemaphoreType.DMA((6,)),
        pltpu.SemaphoreType.DMA((6,)),
    ]
    gs_shape, gt_shape = (9 * ch, ch), (3 * ch, ch)
    if inside:
        gs_shape, gt_shape = (2 * SPATIAL_ROWS, LANES), (2 * TEMPORAL_ROWS, LANES)
        for _, _, a, b in CHUNKS:
            n = a + b
            scratch += [pltpu.VMEM((16, n, LANES), BF16)] * 2
            scratch += [pltpu.VMEM((16, n, LANES), F32)]
            scratch += [pltpu.VMEM((8, a, LANES), BF16)] * 2
            scratch += [pltpu.VMEM((8, b, LANES), BF16)] * 2
            scratch += [pltpu.VMEM((4, a, LANES), BF16)] * 2
            scratch += [pltpu.VMEM((4, b, LANES), BF16)] * 2
        for _, _, a, b in CHUNKS:
            n = a + b
            scratch += [
                pltpu.VMEM((4, n, LANES), F32),
                pltpu.VMEM((4, n, LANES), BF16),
                pltpu.VMEM((3, n, LANES), BF16),
            ]
        scratch += [pltpu.SemaphoreType.DMA((8 * len(CHUNKS),))] * 2
    out, gclip, gs, gt = pl.pallas_call(
        functools.partial(body, sizes, inside),
        out_shape=(
            jax.ShapeDtypeStruct(clip.shape, BF16),
            jax.ShapeDtypeStruct(clip.shape, BF16),
            jax.ShapeDtypeStruct(gs_shape, F32),
            jax.ShapeDtypeStruct(gt_shape, F32),
        ),
        in_specs=[pl.BlockSpec(memory_space=pltpu.HBM)] * 4,
        out_specs=(pl.BlockSpec(memory_space=pltpu.HBM),) * 2 + (vmem,) * 2,
        scratch_shapes=scratch,
        compiler_params=pltpu.CompilerParams(
            collective_id=0, has_side_effects=True, vmem_limit_bytes=125 * 1024 * 1024 // 2
        ),
        name="section",
    )(clip, cot, sw, tw)
    gs, gt = gs.reshape(-1), gt.reshape(-1)
    if not inside:
        gs, gt = (
            lax.psum_scatter(gs, ("tm", "height"), scatter_dimension=0, tiled=True),
            lax.psum_scatter(gt, ("tm", "height"), scatter_dimension=0, tiled=True),
        )
    return out, gclip, gs, gt


def solution(mesh):
    sizes = (mesh.shape["tm"], mesh.shape["height"])
    return jax.shard_map(
        functools.partial(shards, sizes),
        mesh=mesh,
        in_specs=(P("tm", "height", None, None), P("tm", "height", None, None), P(), P()),
        out_specs=(
            P("tm", "height", None, None),
            P("tm", "height", None, None),
            P(("tm", "height")),
            P(("tm", "height")),
        ),
        check_vma=False,
    )
```

time: 40.3 us -> 35.9 us (0.89)
  Pallas kernels: 32.6 us -> 29.6 us
  local copies, waits for them, and re-layouts: 6.85 us -> 5.48 us
    pallas_call x1, Pallas kernels: 32.6 us -> 29.6 us  [shards(): pl.pallas_call(functools.partial(body, sizes, inside), out_shape=(jax.Sha...]
    unnamed x12 -> x6, local copies, waits for them, and re-layouts: 6.85 us -> 5.48 us
where the time goes in v2:
time: 35.9 us; the launch traced here: 35.7 us
  Pallas kernels  29.6 us (82%)
  local copies, waits for them, and re-layouts  5.48 us (15%)
  between operations  0.65 us (2%)
    pallas_call x1, Pallas kernels, shards(): pl.pallas_call(functools.partial(body, sizes, inside), out_shape=(jax.Sha...  29.6 us
    unnamed x6, local copies, waits for them, and re-layouts  5.48 us

profile of v2, /device:TPU:0, one launch (start us, length us, event | category | flops | bytes accessed | tf_op | source)
XLA Modules:
  0.0 35.7 jit_solution(12997297582362661076)
XLA Ops:
  0.6 29.6 %section.1 = (bf16[2,4,64,256]{3,2,1,0:T(8,128)(2,1)}, bf16[2,4,64,256]{3,2,1,0:T(8,128)(2,1)}, f32[144,128]{1,0:T(8,128)}, f32[48,128]{1,0:T(8,128)}) custom-call(bf16[2,4,64,256]{3,2,1,0:T(8,128)(2,1)} %clip_hbm.1, bf16[2,4,64,256]{3,2,1,0:T(8,128)(2,1)} %cot_hbm.1, bf16[3,3,256,256]{3,2,1,0:T(8,128)(2,1)} %sw_hbm.1, bf16[3,256,256]{2,1,0:T(8,128)(2,1)} %tw_hbm.1), custom_call_target="tpu_custom_call" | custom-call | tf_op jit(solution)/shard_map/section/pallas_call | solution.py:463
  30.2 0.0 copy-start
  30.2 1.7 %copy.12 = bf16[2,4,64,256]{3,2,1,0:T(8,128)(2,1)} copy(bf16[2,4,64,256]{3,2,1,0:T(8,128)(2,1)} %get-tuple-element.16) | data formatting | bytes 524288
  31.9 1.7 %copy.13 = bf16[2,4,64,256]{3,2,1,0:T(8,128)(2,1)} copy(bf16[2,4,64,256]{3,2,1,0:T(8,128)(2,1)} %get-tuple-element.17) | data formatting | bytes 524288
  33.6 1.5 %copy.14 = f32[18432]{0:T(1024)} copy(f32[18432]{0:T(1024)} %bitcast.2) | data formatting | bytes 147456
  35.1 0.0 copy-done
  35.1 0.6 %copy.15 = f32[6144]{0:T(1024)} copy(f32[6144]{0:T(1024)S(1)} %bitcast.3) | data formatting | bytes 49152
Async XLA Ops:
  30.2 4.9 %copy-start = (f32[48,128]{1,0:T(8,128)S(1)}, f32[48,128]{1,0:T(8,128)}, u32[]{:S(2)}) copy-start(f32[48,128]{1,0:T(8,128)} %get-tuple-element.11) | copy-start | bytes 73732

commit v3 on v2

--- a/solution.py
+++ b/solution.py
@@ -48,14 +48,18 @@
 
 def body(
     sizes, reduce_inside, clip_hbm, cot_hbm, sw_hbm, tw_hbm, out_hbm, gclip_hbm, gs_out, gt_out,
-    clip, cot, sw, tw, out, gclip, in_sem, out_sem,
-    clip_halo, cot_next, mid_prev, mid, gm, gm_halo, act3, gm3, act_t, gs, gt, hsend, hrecv, *rest
+    clip, sw, tw, out, gclip, in_sem, out_sem,
+    clip_halo, cot_ext, mid_ext, mid_t, gm, gm_halo, act3, gm3, act_t, grad_act, gs, gt, hsend, hrecv, *rest
 ):
     tm_count, h_count = sizes
     frames, rows, cols, ch = clip.shape
+    block = (frames, rows, cols, ch)
     tm = lax.axis_index("tm")
     hh = lax.axis_index("height")
     cells = rows * cols
+
+    cot, cot_next = cot_ext.at[pl.ds(0, frames)], cot_ext.at[pl.ds(frames, frames)]
+    mid_prev, mid = mid_ext.at[pl.ds(0, frames)], mid_ext.at[pl.ds(frames, frames)]
 
     loads = [
         pltpu.make_async_copy(src, dst, in_sem.at[i])
@@ -149,18 +153,17 @@
         put_act(f, rows + 1, clip_halo[1, f])
 
     loads[2].wait()
-    for f in range(frames):
-        total = None
-        for r in range(3):
-            term = dot(flat(act3[f, r : r + rows]), flat(sw[r]))
-            total = term if total is None else total + term
-        mid[f] = total.astype(BF16).reshape(rows, cols, ch)
+    total = None
+    for r in range(3):
+        term = dot(flat(act3[:, r : r + rows]), flat(sw[r]))
+        total = term if total is None else total + term
+    mid_ext[frames:] = total.astype(BF16).reshape(block)
     mid_copy = (copy(mid, mid_prev, 3, after), has_after, has_before)
     start(mid_copy)
 
     for r in range(3):
         for f in range(frames):
-            act_t[r, :, pl.ds(f * cells, cells)] = flat(
+            act_t[pl.ds(r * ch, ch), pl.ds(f * cells, cells)] = flat(
                 act3[f, r : r + rows, :, pl.ds(ch, ch)]
             ).T
 
@@ -173,58 +176,51 @@
         for q in range(3):
             gm3[f, row, :, pl.ds(q * ch, ch)] = shifts[2 - q]
 
-    def future(t):
-        return cot[t] if t < frames else cot_next[t - frames]
-
-    for f in range(frames):
-        total = None
-        for k in range(3):
-            term = dot(flat(future(f + k)), tw[k], NT)
-            total = term if total is None else total + term
-        value = total.astype(BF16).reshape(rows, cols, ch)
-        gm[f] = value
-        for row in range(rows):
-            put_gm(f, row + 1, value[row])
+    total = None
+    for k in range(3):
+        term = dot(flat(cot_ext[k : k + frames]), tw[k], NT)
+        total = term if total is None else total + term
+    value = total.astype(BF16).reshape(block)
+    gm[...] = value
     gm_up, gm_down = exchange(4, gm.at[:, 0], gm.at[:, rows - 1], gm_halo, up, down)
     start(gm_up)
     start(gm_down)
-
-    for r in range(3):
-        total = None
-        for f in range(frames):
-            term = dot(
-                act_t[r, :, pl.ds(f * cells, cells)], flat(gm3[f, 1 : 1 + rows])
-            )
-            total = term if total is None else total + term
-        for q in range(3):
-            gs[pl.ds((r * 3 + q) * ch, ch), :] = total[:, q * ch : (q + 1) * ch]
-
-    def history(t):
-        return mid[t] if t >= 0 else mid_prev[frames + t]
+    for f in range(frames):
+        for row in range(rows):
+            put_gm(f, row + 1, value[f, row])
+
+    for q in range(3):
+        total = dot(act_t[...], flat(gm3[:, 1 : 1 + rows, :, pl.ds(q * ch, ch)]))
+        for r in range(3):
+            gs[pl.ds((r * 3 + q) * ch, ch), :] = total[r * ch : (r + 1) * ch]
+
+    def turn_mid(t):
+        mid_t[:, pl.ds(t * cells, cells)] = flat(mid_ext[t]).T
 
     def do_temporal():
+        for t in range(frames, 2 * frames):
+            turn_mid(t)
         wait_recv(mid_copy, mid_prev)
-        turned = {t: flat(history(t)).T for t in range(-2, frames)}
-        for k in range(3):
-            total = None
-            for f in range(frames):
-                term = dot(turned[f - k], flat(cot[f]))
-                total = term if total is None else total + term
-            gt[pl.ds(k * ch, ch), :] = total
+        for t in range(frames):
+            turn_mid(t)
+        left = jnp.concatenate(
+            [mid_t[:, pl.ds((frames - k) * cells, frames * cells)] for k in range(3)], axis=0
+        )
+        gt[...] = dot(left, flat(cot_ext[:frames]))
 
     stores = []
 
-    def store(src, dst, f, slot):
-        c = pltpu.make_async_copy(src.at[f], dst.at[f], out_sem.at[slot])
+    def store(src, dst, slot):
+        c = pltpu.make_async_copy(src, dst, out_sem.at[slot])
         c.start()
         stores.append(c)
 
-    def do_output(f):
-        total = flat(clip[f]).astype(F32)
+    def do_output():
+        total = flat(clip[...]).astype(F32)
         for k in range(3):
-            total = total + dot(flat(history(f - k)), tw[k])
-        out[f] = total.astype(BF16).reshape(rows, cols, ch)
-        store(out, out_hbm, f, f)
+            total = total + dot(flat(mid_ext[frames - k : 2 * frames - k]), tw[k])
+        out[...] = total.astype(BF16).reshape(block)
+        store(out, out_hbm, 0)
 
     def do_gm_halo():
         wait_recv(gm_up, gm_halo.at[1])
@@ -233,31 +229,37 @@
             put_gm(f, 0, gm_halo[0, f])
             put_gm(f, rows + 1, gm_halo[1, f])
 
-    def do_grad_clip(f):
+    def do_grad_act():
         total = None
         for r in range(3):
             for q in range(3):
-                left = flat(gm3[f, 2 - r : 2 - r + rows, :, pl.ds(q * ch, ch)])
+                left = flat(gm3[:, 2 - r : 2 - r + rows, :, pl.ds(q * ch, ch)])
                 term = dot(left, sw[r, q], NT)
                 total = term if total is None else total + term
-        values = flat(clip[f]).astype(F32)
-        scale_inv = lax.rsqrt(jnp.mean(values * values, axis=-1, keepdims=True) + EPSILON)
-        normed = values * scale_inv
-        gate = 1.0 / (1.0 + jnp.exp(-normed))
-        inner = total * (gate * (1.0 + normed * (1.0 - gate)))
-        slope = scale_inv * (inner - normed * jnp.mean(inner * normed, axis=-1, keepdims=True))
-        gclip[f] = (flat(cot[f]).astype(F32) + slope).astype(BF16).reshape(rows, cols, ch)
-        store(gclip, gclip_hbm, f, frames + f)
+        grad_act[...] = total
+
+    def do_grad_clip():
+        for f in range(frames):
+            values = flat(clip[f]).astype(F32)
+            scale_inv = lax.rsqrt(jnp.mean(values * values, axis=-1, keepdims=True) + EPSILON)
+            normed = values * scale_inv
+            gate = 1.0 / (1.0 + jnp.exp(-normed))
+            inner = grad_act[pl.ds(f * cells, cells), :] * (gate * (1.0 + normed * (1.0 - gate)))
+            slope = scale_inv * (
+                inner - normed * jnp.mean(inner * normed, axis=-1, keepdims=True)
+            )
+            total = flat(cot_ext[f]).astype(F32) + slope
+            gclip[f] = total.astype(BF16).reshape(rows, cols, ch)
+        store(gclip, gclip_hbm, 1)
 
     scale = 1.0 / math.sqrt(frames * tm_count * rows * h_count * cols)
 
     if not reduce_inside:
         do_temporal()
-        for f in range(frames):
-            do_output(f)
+        do_output()
         do_gm_halo()
-        for f in range(frames):
-            do_grad_clip(f)
+        do_grad_act()
+        do_grad_clip()
         gs_out[...] = gs[...] * scale
         gt_out[...] = gt[...] * scale
     else:
@@ -396,13 +398,12 @@
                 flight[i] = stage(i)
 
         advance(stage_one)
-        do_output(0)
-        do_output(1)
+        do_output()
         do_gm_halo()
         advance(stage_two)
-        do_grad_clip(0)
+        do_grad_act()
         advance(stage_z)
-        do_grad_clip(1)
+        do_grad_clip()
         done = []
         for i in range(len(CHUNKS)):
             finish(flight[i])
@@ -414,6 +415,30 @@
         wait_send(c)
     for c in stores:
         c.wait()
+
+
+def hand_on(*refs):
+    count = len(refs) // 2
+    copies = [
+        pltpu.make_async_copy(refs[i], refs[count + i], refs[-1].at[i]) for i in range(count)
+    ]
+    for c in copies:
+        c.start()
+    for c in copies:
+        c.wait()
+
+
+def handed_on(*arrays):
+    place = pl.BlockSpec(memory_space=pltpu.HBM)
+    return pl.pallas_call(
+        hand_on,
+        out_shape=tuple(jax.ShapeDtypeStruct(x.shape, x.dtype) for x in arrays),
+        in_specs=[place] * len(arrays),
+        out_specs=(place,) * len(arrays),
+        scratch_shapes=[pltpu.SemaphoreType.DMA((len(arrays),))],
+        compiler_params=pltpu.CompilerParams(vmem_limit_bytes=125 * 1024 * 1024 // 2),
+        name="hand_on",
+    )(*arrays)
 
 
 def shards(sizes, clip, cot, sw, tw):
@@ -423,19 +448,20 @@
     wide = (frames, rows + 2, cols, 3 * ch)
     edge = (2, frames, cols, ch)
     vmem = pl.BlockSpec(memory_space=pltpu.VMEM)
-    scratch = [pltpu.VMEM(x.shape, x.dtype) for x in (clip, cot, sw, tw, clip, clip)]
+    scratch = [pltpu.VMEM(x.shape, x.dtype) for x in (clip, sw, tw, clip, clip)]
     scratch += [
         pltpu.SemaphoreType.DMA((4,)),
-        pltpu.SemaphoreType.DMA((2 * frames,)),
+        pltpu.SemaphoreType.DMA((2,)),
         pltpu.VMEM(edge, BF16),
-        pltpu.VMEM(clip.shape, BF16),
-        pltpu.VMEM(clip.shape, BF16),
-        pltpu.VMEM(clip.shape, BF16),
+        pltpu.VMEM((2 * frames, rows, cols, ch), BF16),
+        pltpu.VMEM((2 * frames, rows, cols, ch), BF16),
+        pltpu.VMEM((ch, 2 * frames * rows * cols), BF16),
         pltpu.VMEM(clip.shape, BF16),
         pltpu.VMEM(edge, BF16),
         pltpu.VMEM(wide, BF16),
         pltpu.VMEM(wide, BF16),
-        pltpu.VMEM((3, ch, frames * rows * cols), BF16),
+        pltpu.VMEM((3 * ch, frames * rows * cols), BF16),
+        pltpu.VMEM((frames * rows * cols, ch), F32),
         pltpu.VMEM((9 * ch, ch), F32),
         pltpu.VMEM((3 * ch, ch), F32),
         pltpu.SemaphoreType.DMA((6,)),
@@ -476,6 +502,8 @@
         ),
         name="section",
     )(clip, cot, sw, tw)
+    if inside:
+        out, gclip, gs, gt = handed_on(out, gclip, gs, gt)
     gs, gt = gs.reshape(-1), gt.reshape(-1)
     if not inside:
         gs, gt = (

time: 35.9 us -> 51.5 us (1.43)
  Pallas kernels: 29.6 us -> 50.7 us
  local copies, waits for them, and re-layouts: 5.48 us -> 0 us
    pallas_call x0 -> x1, Pallas kernels: none -> 20 us  [handed_on(): pl.pallas_call(hand_on, out_shape=tuple((jax.ShapeDtypeStruct(x.shape, x....]
    unnamed x6 -> x0, local copies, waits for them, and re-layouts: 5.48 us -> none
    pallas_call x1, Pallas kernels: 29.6 us -> 30.7 us  [shards(): pl.pallas_call(functools.partial(body, sizes, inside), out_shape=(jax.Sha...]
where the time goes in v3:
time: 51.5 us; the launch traced here: 51.4 us
  Pallas kernels  50.7 us (98%)
  between operations  0.64 us (1%)
    pallas_call x1, Pallas kernels, shards(): pl.pallas_call(functools.partial(body, sizes, inside), out_shape=(jax.Sha...  30.7 us
    pallas_call x1, Pallas kernels, handed_on(): pl.pallas_call(hand_on, out_shape=tuple((jax.ShapeDtypeStruct(x.shape, x....  20 us

profile of v3, /device:TPU:0, one launch (start us, length us, event | category | flops | bytes accessed | tf_op | source)
XLA Modules:
  0.0 51.4 jit_solution(6291791009230260498)
XLA Ops:
  0.6 30.7 %section.1 = (bf16[2,4,64,256]{3,2,1,0:T(8,128)(2,1)}, bf16[2,4,64,256]{3,2,1,0:T(8,128)(2,1)}, f32[144,128]{1,0:T(8,128)}, f32[48,128]{1,0:T(8,128)}) custom-call(bf16[2,4,64,256]{3,2,1,0:T(8,128)(2,1)} %clip_hbm.1, bf16[2,4,64,256]{3,2,1,0:T(8,128)(2,1)} %cot_hbm.1, bf16[3,3,256,256]{3,2,1,0:T(8,128)(2,1)} %sw_hbm.1, bf16[3,256,256]{2,1,0:T(8,128)(2,1)} %tw_hbm.1), custom_call_target="tpu_custom_call" | custom-call | tf_op jit(solution)/shard_map/section/pallas_call | solution.py:489
  31.4 20.0 %hand_on.1 = (bf16[2,4,64,256]{3,2,1,0:T(8,128)(2,1)}, bf16[2,4,64,256]{3,2,1,0:T(8,128)(2,1)}, f32[144,128]{1,0:T(8,128)}, f32[48,128]{1,0:T(8,128)}) custom-call(bf16[2,4,64,256]{3,2,1,0:T(8,128)(2,1)} %get-tuple-element.12.refs_0_, bf16[2,4,64,256]{3,2,1,0:T(8,128)(2,1)} %get-tuple-element.13.refs_1_, f32[144,128]{1,0:T(8,128)} %get-tuple-element.14.refs_2_, ...), custom_call_target="tpu_custom_call" | custom-call | tf_op jit(solution)/shard_map/hand_on/pallas_call | solution.py:433

commit v4 on v3

--- a/solution.py
+++ b/solution.py
@@ -47,8 +47,8 @@
 
 
 def body(
-    sizes, reduce_inside, clip_hbm, cot_hbm, sw_hbm, tw_hbm, out_hbm, gclip_hbm, gs_out, gt_out,
-    clip, sw, tw, out, gclip, in_sem, out_sem,
+    sizes, reduce_inside, clip_hbm, cot_hbm, sw_hbm, tw_hbm, out, gclip, gs_out, gt_out,
+    clip, sw, tw, in_sem,
     clip_halo, cot_ext, mid_ext, mid_t, gm, gm_halo, act3, gm3, act_t, grad_act, gs, gt, hsend, hrecv, *rest
 ):
     tm_count, h_count = sizes
@@ -208,19 +208,11 @@
         )
         gt[...] = dot(left, flat(cot_ext[:frames]))
 
-    stores = []
-
-    def store(src, dst, slot):
-        c = pltpu.make_async_copy(src, dst, out_sem.at[slot])
-        c.start()
-        stores.append(c)
-
     def do_output():
         total = flat(clip[...]).astype(F32)
         for k in range(3):
             total = total + dot(flat(mid_ext[frames - k : 2 * frames - k]), tw[k])
         out[...] = total.astype(BF16).reshape(block)
-        store(out, out_hbm, 0)
 
     def do_gm_halo():
         wait_recv(gm_up, gm_halo.at[1])
@@ -229,14 +221,16 @@
             put_gm(f, 0, gm_halo[0, f])
             put_gm(f, rows + 1, gm_halo[1, f])
 
-    def do_grad_act():
+    def do_grad_act(r):
         total = None
-        for r in range(3):
-            for q in range(3):
-                left = flat(gm3[:, 2 - r : 2 - r + rows, :, pl.ds(q * ch, ch)])
-                term = dot(left, sw[r, q], NT)
-                total = term if total is None else total + term
-        grad_act[...] = total
+        for q in range(3):
+            left = flat(gm3[:, 2 - r : 2 - r + rows, :, pl.ds(q * ch, ch)])
+            term = dot(left, sw[r, q], NT)
+            total = term if total is None else total + term
+        if r == 0:
+            grad_act[...] = total
+        else:
+            grad_act[...] += total
 
     def do_grad_clip():
         for f in range(frames):
@@ -250,7 +244,6 @@
             )
             total = flat(cot_ext[f]).astype(F32) + slope
             gclip[f] = total.astype(BF16).reshape(rows, cols, ch)
-        store(gclip, gclip_hbm, 1)
 
     scale = 1.0 / math.sqrt(frames * tm_count * rows * h_count * cols)
 
@@ -258,7 +251,8 @@
         do_temporal()
         do_output()
         do_gm_halo()
-        do_grad_act()
+        for r in range(3):
+            do_grad_act(r)
         do_grad_clip()
         gs_out[...] = gs[...] * scale
         gt_out[...] = gt[...] * scale
@@ -400,9 +394,11 @@
         advance(stage_one)
         do_output()
         do_gm_halo()
+        do_grad_act(0)
         advance(stage_two)
-        do_grad_act()
+        do_grad_act(1)
         advance(stage_z)
+        do_grad_act(2)
         do_grad_clip()
         done = []
         for i in range(len(CHUNKS)):
@@ -413,8 +409,6 @@
 
     for c in (clip_up, clip_down, cot_copy, mid_copy, gm_up, gm_down):
         wait_send(c)
-    for c in stores:
-        c.wait()
 
 
 def hand_on(*refs):
@@ -433,10 +427,10 @@
     return pl.pallas_call(
         hand_on,
         out_shape=tuple(jax.ShapeDtypeStruct(x.shape, x.dtype) for x in arrays),
-        in_specs=[place] * len(arrays),
+        in_specs=[pl.BlockSpec(memory_space=pltpu.VMEM)] * len(arrays),
         out_specs=(place,) * len(arrays),
         scratch_shapes=[pltpu.SemaphoreType.DMA((len(arrays),))],
-        compiler_params=pltpu.CompilerParams(vmem_limit_bytes=125 * 1024 * 1024 // 2),
+        compiler_params=pltpu.CompilerParams(vmem_limit_bytes=4 * 1024 * 1024),
         name="hand_on",
     )(*arrays)
 
@@ -448,10 +442,9 @@
     wide = (frames, rows + 2, cols, 3 * ch)
     edge = (2, frames, cols, ch)
     vmem = pl.BlockSpec(memory_space=pltpu.VMEM)
-    scratch = [pltpu.VMEM(x.shape, x.dtype) for x in (clip, sw, tw, clip, clip)]
+    scratch = [pltpu.VMEM(x.shape, x.dtype) for x in (clip, sw, tw)]
     scratch += [
         pltpu.SemaphoreType.DMA((4,)),
-        pltpu.SemaphoreType.DMA((2,)),
         pltpu.VMEM(edge, BF16),
         pltpu.VMEM((2 * frames, rows, cols, ch), BF16),
         pltpu.VMEM((2 * frames, rows, cols, ch), BF16),
@@ -495,10 +488,10 @@
             jax.ShapeDtypeStruct(gt_shape, F32),
         ),
         in_specs=[pl.BlockSpec(memory_space=pltpu.HBM)] * 4,
-        out_specs=(pl.BlockSpec(memory_space=pltpu.HBM),) * 2 + (vmem,) * 2,
+        out_specs=(vmem,) * 4,
         scratch_shapes=scratch,
         compiler_params=pltpu.CompilerParams(
-            collective_id=0, has_side_effects=True, vmem_limit_bytes=125 * 1024 * 1024 // 2
+            collective_id=0, has_side_effects=True, vmem_limit_bytes=531 * 1024 * 1024 // 10
         ),
         name="section",
     )(clip, cot, sw, tw)

time: 51.5 us -> 31.1 us (0.60)
  Pallas kernels: 50.7 us -> 30.3 us
    pallas_call x1, Pallas kernels: 20 us -> 0.84 us  [handed_on(): pl.pallas_call(hand_on, out_shape=tuple((jax.ShapeDtypeStruct(x.shape, x....]
    pallas_call x1, Pallas kernels: 30.7 us -> 29.5 us  [shards(): pl.pallas_call(functools.partial(body, sizes, inside), out_shape=(jax.Sha...]
where the time goes in v4:
time: 31.1 us; the launch traced here: 31 us
  Pallas kernels  30.3 us (97%)
  between operations  0.64 us (2%)
    pallas_call x1, Pallas kernels, shards(): pl.pallas_call(functools.partial(body, sizes, inside), out_shape=(jax.Sha...  29.5 us
    pallas_call x1, Pallas kernels, handed_on(): pl.pallas_call(hand_on, out_shape=tuple((jax.ShapeDtypeStruct(x.shape, x....  0.84 us

profile of v4, /device:TPU:0, one launch (start us, length us, event | category | flops | bytes accessed | tf_op | source)
XLA Modules:
  0.0 31.0 jit_solution(6013696690870124444)
XLA Ops:
  0.6 29.5 %section.1 = (bf16[2,4,64,256]{3,2,1,0:T(8,128)(2,1)S(1)}, bf16[2,4,64,256]{3,2,1,0:T(8,128)(2,1)S(1)}, f32[144,128]{1,0:T(8,128)S(1)}, f32[48,128]{1,0:T(8,128)S(1)}) custom-call(bf16[2,4,64,256]{3,2,1,0:T(8,128)(2,1)} %clip_hbm.1, bf16[2,4,64,256]{3,2,1,0:T(8,128)(2,1)} %cot_hbm.1, bf16[3,3,256,256]{3,2,1,0:T(8,128)(2,1)} %sw_hbm.1, ...), custom_call_target="tpu_custom_call" | custom-call | tf_op jit(solution)/shard_map/section/pallas_call | solution.py:482
  30.1 0.8 %hand_on.1 = (bf16[2,4,64,256]{3,2,1,0:T(8,128)(2,1)}, bf16[2,4,64,256]{3,2,1,0:T(8,128)(2,1)}, f32[144,128]{1,0:T(8,128)}, f32[48,128]{1,0:T(8,128)}) custom-call(bf16[2,4,64,256]{3,2,1,0:T(8,128)(2,1)S(1)} %get-tuple-element.12.refs_0_, bf16[2,4,64,256]{3,2,1,0:T(8,128)(2,1)S(1)} %get-tuple-element.13.refs_1_, f32[144,128]{1,0:T(8,128)S(1)} %get-tuple-element.14.refs_2_, ...), custom_call_target="tpu_custom_call" | custom-call | tf_op jit(solution)/shard_map/hand_on/pallas_call | solution.py:427

commit v5 on v4

--- a/solution.py
+++ b/solution.py
@@ -146,6 +146,14 @@
     for f in range(frames):
         for row in range(rows):
             put_act(f, row + 1, clip[f, row])
+
+    def turn_act(r):
+        for f in range(frames):
+            act_t[pl.ds(r * ch, ch), pl.ds(f * cells, cells)] = flat(
+                act3[f, r : r + rows, :, pl.ds(ch, ch)]
+            ).T
+
+    turn_act(1)
     wait_recv(clip_up, clip_halo.at[1])
     wait_recv(clip_down, clip_halo.at[0])
     for f in range(frames):
@@ -161,11 +169,8 @@
     mid_copy = (copy(mid, mid_prev, 3, after), has_after, has_before)
     start(mid_copy)
 
-    for r in range(3):
-        for f in range(frames):
-            act_t[pl.ds(r * ch, ch), pl.ds(f * cells, cells)] = flat(
-                act3[f, r : r + rows, :, pl.ds(ch, ch)]
-            ).T
+    turn_act(0)
+    turn_act(2)
 
     loads[1].wait()
     loads[3].wait()
@@ -232,18 +237,17 @@
         else:
             grad_act[...] += total
 
-    def do_grad_clip():
-        for f in range(frames):
-            values = flat(clip[f]).astype(F32)
-            scale_inv = lax.rsqrt(jnp.mean(values * values, axis=-1, keepdims=True) + EPSILON)
-            normed = values * scale_inv
-            gate = 1.0 / (1.0 + jnp.exp(-normed))
-            inner = grad_act[pl.ds(f * cells, cells), :] * (gate * (1.0 + normed * (1.0 - gate)))
-            slope = scale_inv * (
-                inner - normed * jnp.mean(inner * normed, axis=-1, keepdims=True)
-            )
-            total = flat(cot_ext[f]).astype(F32) + slope
-            gclip[f] = total.astype(BF16).reshape(rows, cols, ch)
+    def do_grad_clip(f):
+        values = flat(clip[f]).astype(F32)
+        scale_inv = lax.rsqrt(jnp.mean(values * values, axis=-1, keepdims=True) + EPSILON)
+        normed = values * scale_inv
+        gate = 1.0 / (1.0 + jnp.exp(-normed))
+        inner = grad_act[pl.ds(f * cells, cells), :] * (gate * (1.0 + normed * (1.0 - gate)))
+        slope = scale_inv * (
+            inner - normed * jnp.mean(inner * normed, axis=-1, keepdims=True)
+        )
+        total = flat(cot_ext[f]).astype(F32) + slope
+        gclip[f] = total.astype(BF16).reshape(rows, cols, ch)
 
     scale = 1.0 / math.sqrt(frames * tm_count * rows * h_count * cols)
 
@@ -253,7 +257,8 @@
         do_gm_halo()
         for r in range(3):
             do_grad_act(r)
-        do_grad_clip()
+        for f in range(frames):
+            do_grad_clip(f)
         gs_out[...] = gs[...] * scale
         gt_out[...] = gt[...] * scale
     else:
@@ -386,20 +391,26 @@
         do_temporal()
         flight[2] = stage_core(2)
 
-        def advance(stage):
-            for i in range(len(CHUNKS)):
-                finish(flight[i])
-                flight[i] = stage(i)
-
-        advance(stage_one)
+        def advance(i, stage):
+            finish(flight[i])
+            flight[i] = stage(i)
+
+        for i in range(len(CHUNKS)):
+            advance(i, stage_one)
         do_output()
         do_gm_halo()
+        advance(0, stage_two)
         do_grad_act(0)
-        advance(stage_two)
+        advance(1, stage_two)
         do_grad_act(1)
-        advance(stage_z)
+        advance(2, stage_two)
+        advance(0, stage_z)
         do_grad_act(2)
-        do_grad_clip()
+        advance(1, stage_z)
+        do_grad_clip(0)
+        advance(2, stage_z)
+        for f in range(1, frames):
+            do_grad_clip(f)
         done = []
         for i in range(len(CHUNKS)):
             finish(flight[i])

time: 31.1 us -> 31.1 us (level)
  no operation moved by 1% of the time
where the time goes in v5:
time: 31.1 us; the launch traced here: 31 us
  Pallas kernels  30.3 us (97%)
  between operations  0.64 us (2%)
    pallas_call x1, Pallas kernels, shards(): pl.pallas_call(functools.partial(body, sizes, inside), out_shape=(jax.Sha...  29.5 us
    pallas_call x1, Pallas kernels, handed_on(): pl.pallas_call(hand_on, out_shape=tuple((jax.ShapeDtypeStruct(x.shape, x....  0.84 us

profile of v5, /device:TPU:0, one launch (start us, length us, event | category | flops | bytes accessed | tf_op | source)
XLA Modules:
  0.0 31.0 jit_solution(80743584159138275)
XLA Ops:
  0.6 29.5 %section.1 = (bf16[2,4,64,256]{3,2,1,0:T(8,128)(2,1)S(1)}, bf16[2,4,64,256]{3,2,1,0:T(8,128)(2,1)S(1)}, f32[144,128]{1,0:T(8,128)S(1)}, f32[48,128]{1,0:T(8,128)S(1)}) custom-call(bf16[2,4,64,256]{3,2,1,0:T(8,128)(2,1)} %clip_hbm.1, bf16[2,4,64,256]{3,2,1,0:T(8,128)(2,1)} %cot_hbm.1, bf16[3,3,256,256]{3,2,1,0:T(8,128)(2,1)} %sw_hbm.1, ...), custom_call_target="tpu_custom_call" | custom-call | tf_op jit(solution)/shard_map/section/pallas_call | solution.py:493
  30.1 0.8 %hand_on.1 = (bf16[2,4,64,256]{3,2,1,0:T(8,128)(2,1)}, bf16[2,4,64,256]{3,2,1,0:T(8,128)(2,1)}, f32[144,128]{1,0:T(8,128)}, f32[48,128]{1,0:T(8,128)}) custom-call(bf16[2,4,64,256]{3,2,1,0:T(8,128)(2,1)S(1)} %get-tuple-element.12.refs_0_, bf16[2,4,64,256]{3,2,1,0:T(8,128)(2,1)S(1)} %get-tuple-element.13.refs_1_, f32[144,128]{1,0:T(8,128)S(1)} %get-tuple-element.14.refs_2_, ...), custom_call_target="tpu_custom_call" | custom-call | tf_op jit(solution)/shard_map/hand_on/pallas_call | solution.py:438

commit v6 on v5

--- a/solution.py
+++ b/solution.py
@@ -19,7 +19,7 @@
 SPATIAL_ROWS = 72
 TEMPORAL_ROWS = 24
 LANES = 128
-CHUNKS = (("spatial", 0, 32, 32), ("spatial", 64, 32, 48), ("temporal", 0, 32, 16))
+CHUNKS = (("spatial", 0, 64, 80), ("temporal", 0, 32, 16))
 
 
 def dot(left, right, dims=NN):
@@ -386,37 +386,34 @@
             ref[pl.ds(0, count, stride=2), :] = value[:count]
             ref[pl.ds(1, count, stride=2), :] = value[count:]
 
-        spatial = (0, 1)
-        flight = {i: stage_core(i) for i in spatial}
+        flight = {0: stage_core(0)}
         do_temporal()
-        flight[2] = stage_core(2)
+        flight[1] = stage_core(1)
 
         def advance(i, stage):
             finish(flight[i])
             flight[i] = stage(i)
 
-        for i in range(len(CHUNKS)):
-            advance(i, stage_one)
+        advance(0, stage_one)
+        advance(1, stage_one)
         do_output()
         do_gm_halo()
+        do_grad_act(0)
         advance(0, stage_two)
-        do_grad_act(0)
+        do_grad_act(1)
         advance(1, stage_two)
-        do_grad_act(1)
-        advance(2, stage_two)
         advance(0, stage_z)
         do_grad_act(2)
+        do_grad_clip(0)
         advance(1, stage_z)
-        do_grad_clip(0)
-        advance(2, stage_z)
         for f in range(1, frames):
             do_grad_clip(f)
         done = []
         for i in range(len(CHUNKS)):
             finish(flight[i])
             done.append(final(i))
-        place(gs_out, jnp.concatenate(done[:2], axis=0), SPATIAL_ROWS)
-        place(gt_out, done[2], TEMPORAL_ROWS)
+        place(gs_out, done[0], SPATIAL_ROWS)
+        place(gt_out, done[1], TEMPORAL_ROWS)
 
     for c in (clip_up, clip_down, cot_copy, mid_copy, gm_up, gm_down):
         wait_send(c)

time: 31.1 us -> 31.6 us (1.016)
  Pallas kernels: 30.3 us -> 30.9 us
    pallas_call x1, Pallas kernels: 29.5 us -> 30 us  [shards(): pl.pallas_call(functools.partial(body, sizes, inside), out_shape=(jax.Sha...]
where the time goes in v6:
time: 31.6 us; the launch traced here: 31.5 us
  Pallas kernels  30.9 us (98%)
  between operations  0.64 us (2%)
    pallas_call x1, Pallas kernels, shards(): pl.pallas_call(functools.partial(body, sizes, inside), out_shape=(jax.Sha...  30 us
    pallas_call x1, Pallas kernels, handed_on(): pl.pallas_call(hand_on, out_shape=tuple((jax.ShapeDtypeStruct(x.shape, x....  0.84 us

profile of v6, /device:TPU:0, one launch (start us, length us, event | category | flops | bytes accessed | tf_op | source)
XLA Modules:
  0.0 31.5 jit_solution(10641077513761111589)
XLA Ops:
  0.6 30.0 %section.1 = (bf16[2,4,64,256]{3,2,1,0:T(8,128)(2,1)S(1)}, bf16[2,4,64,256]{3,2,1,0:T(8,128)(2,1)S(1)}, f32[144,128]{1,0:T(8,128)S(1)}, f32[48,128]{1,0:T(8,128)S(1)}) custom-call(bf16[2,4,64,256]{3,2,1,0:T(8,128)(2,1)} %clip_hbm.1, bf16[2,4,64,256]{3,2,1,0:T(8,128)(2,1)} %cot_hbm.1, bf16[3,3,256,256]{3,2,1,0:T(8,128)(2,1)} %sw_hbm.1, ...), custom_call_target="tpu_custom_call" | custom-call | tf_op jit(solution)/shard_map/section/pallas_call | solution.py:490
  30.6 0.8 %hand_on.1 = (bf16[2,4,64,256]{3,2,1,0:T(8,128)(2,1)}, bf16[2,4,64,256]{3,2,1,0:T(8,128)(2,1)}, f32[144,128]{1,0:T(8,128)}, f32[48,128]{1,0:T(8,128)}) custom-call(bf16[2,4,64,256]{3,2,1,0:T(8,128)(2,1)S(1)} %get-tuple-element.12.refs_0_, bf16[2,4,64,256]{3,2,1,0:T(8,128)(2,1)S(1)} %get-tuple-element.13.refs_1_, f32[144,128]{1,0:T(8,128)S(1)} %get-tuple-element.14.refs_2_, ...), custom_call_target="tpu_custom_call" | custom-call | tf_op jit(solution)/shard_map/hand_on/pallas_call | solution.py:435

commit v7 on v4

--- a/solution.py
+++ b/solution.py
@@ -19,7 +19,7 @@
 SPATIAL_ROWS = 72
 TEMPORAL_ROWS = 24
 LANES = 128
-CHUNKS = (("spatial", 0, 32, 32), ("spatial", 64, 32, 48), ("temporal", 0, 32, 16))
+CHUNKS = (("spatial", 0, 32, 32), ("spatial", 64, 32, 48), ("temporal", 0, 16, 32))
 
 
 def dot(left, right, dims=NN):

time: 31.1 us -> 31.1 us (level)
  no operation moved by 1% of the time
where the time goes in v7:
time: 31.1 us; the launch traced here: 30.9 us
  Pallas kernels  30.3 us (97%)
  between operations  0.64 us (2%)
    pallas_call x1, Pallas kernels, shards(): pl.pallas_call(functools.partial(body, sizes, inside), out_shape=(jax.Sha...  29.5 us
    pallas_call x1, Pallas kernels, handed_on(): pl.pallas_call(hand_on, out_shape=tuple((jax.ShapeDtypeStruct(x.shape, x....  0.84 us

profile of v7, /device:TPU:0, one launch (start us, length us, event | category | flops | bytes accessed | tf_op | source)
XLA Modules:
  0.0 30.9 jit_solution(2152403225480439891)
XLA Ops:
  0.6 29.5 %section.1 = (bf16[2,4,64,256]{3,2,1,0:T(8,128)(2,1)S(1)}, bf16[2,4,64,256]{3,2,1,0:T(8,128)(2,1)S(1)}, f32[144,128]{1,0:T(8,128)S(1)}, f32[48,128]{1,0:T(8,128)S(1)}) custom-call(bf16[2,4,64,256]{3,2,1,0:T(8,128)(2,1)} %clip_hbm.1, bf16[2,4,64,256]{3,2,1,0:T(8,128)(2,1)} %cot_hbm.1, bf16[3,3,256,256]{3,2,1,0:T(8,128)(2,1)} %sw_hbm.1, ...), custom_call_target="tpu_custom_call" | custom-call | tf_op jit(solution)/shard_map/section/pallas_call | solution.py:482
  30.1 0.8 %hand_on.1 = (bf16[2,4,64,256]{3,2,1,0:T(8,128)(2,1)}, bf16[2,4,64,256]{3,2,1,0:T(8,128)(2,1)}, f32[144,128]{1,0:T(8,128)}, f32[48,128]{1,0:T(8,128)}) custom-call(bf16[2,4,64,256]{3,2,1,0:T(8,128)(2,1)S(1)} %get-tuple-element.12.refs_0_, bf16[2,4,64,256]{3,2,1,0:T(8,128)(2,1)S(1)} %get-tuple-element.13.refs_1_, f32[144,128]{1,0:T(8,128)S(1)} %get-tuple-element.14.refs_2_, ...), custom_call_target="tpu_custom_call" | custom-call | tf_op jit(solution)/shard_map/hand_on/pallas_call | solution.py:427
